TPU v7x, 32 devices: a whole 2x2x4 slice. The times are simulated.
32 devices in a mesh: dp: 4 (over y, core), expert: 8 (over z, x).
Axes of the slice: x: 2, y: 2, z: 4, core: 2. Of those that a mesh axis runs over, the one named last changes fastest.
Arguments:
- tokens: bfloat16 [4096, 7168], P(('dp', 'expert')), may hold values from -6 to 6
- chosen: int32 [8, 288], replicated, may hold values from 0 to 4095, as said below
- combine_fixed: int32 [8, 288], replicated, may hold values from 6554 to 65535
- w_gate: bfloat16 [8, 7168, 2048], P('expert', None, 'dp'), may hold values from -0.0625 to 0.0625
- w_up: bfloat16 [8, 7168, 2048], P('expert', None, 'dp'), may hold values from -0.0625 to 0.0625
- w_down: bfloat16 [8, 2048, 7168], P('expert', 'dp'), may hold values from -0.125 to 0.125
Outputs:
- mixed: bfloat16 [4096, 7168], P(('dp', 'expert'))
Inputs may be any that keep to these rules, and one draw needn't show every extreme that they name: `chosen`: in each row the 288 token numbers differ. Call tokens k * 128 to (k + 1) * 128 - 1 the tokens of device k: a row holds at most 18 tokens of one device, and exactly 18 of some device.
All inputs are finite; a program needn't handle non-finite values.
Results may differ from a plain program's by a relative error of at most 0.015.
Values may be sent and summed in bfloat16 or wider, within the bound.
A program may use at most 128 MiB of HBM per device.

v0:
```python
import jax
import jax.numpy as jnp
from jax import lax
from jax.sharding import PartitionSpec as P


def slot_tables(chosen, tok_count, worker_ordinal):
    owners = chosen // tok_count
    onehot = (
        owners[:, :, None] == jnp.arange(worker_ordinal, dtype=jnp.int32)[None, None, :]
    ).astype(jnp.int32)
    earlier = jnp.cumsum(onehot, axis=1) - onehot
    ranks = jnp.sum(earlier * onehot, axis=2)
    return (owners, ranks)


def shards(tokens, chosen, combine_fixed, w_gate, w_up, w_down):
    dp_count = lax.axis_size("dp")
    ex_count = lax.axis_size("expert")
    worker_ordinal = dp_count * ex_count
    tok_count, model_width = tokens.shape
    expert_total, capacity = chosen.shape
    slot_count = min(tok_count, max(4, 2 * capacity // worker_ordinal))
    my_index = lax.axis_index("dp") * ex_count + lax.axis_index("expert")
    owners, ranks = slot_tables(chosen, tok_count, worker_ordinal)
    local_idx = chosen - owners * tok_count
    is_mine = owners == my_index
    matches = is_mine[:, :, None] & (
        ranks[:, :, None] == jnp.arange(slot_count, dtype=jnp.int32)[None, None, :]
    )
    match_int = matches.astype(jnp.int32)
    source_idx = jnp.sum(match_int * local_idx[:, :, None], axis=1)
    present = jnp.sum(match_int, axis=1)
    scaled = combine_fixed.astype(jnp.float32) / 65536.0
    weights = jnp.sum(matches.astype(jnp.float32) * scaled[:, :, None], axis=1)
    send_rows = jnp.take(tokens, source_idx.reshape(-1), axis=0)
    send_rows = jnp.where(present.reshape(-1, 1) > 0, send_rows, jnp.zeros_like(send_rows))
    send_rows = send_rows.reshape(expert_total, slot_count, model_width)
    my_expert = lax.axis_index("expert")
    my_owners = lax.dynamic_index_in_dim(owners, my_expert, 0, keepdims=False)
    my_ranks = lax.dynamic_index_in_dim(ranks, my_expert, 0, keepdims=False)
    positions = my_owners * slot_count + my_ranks
    spread = jnp.broadcast_to(send_rows[None], (dp_count, expert_total, slot_count, model_width))
    spread = spread.reshape(worker_ordinal, slot_count, model_width)
    arrived = lax.all_to_all(spread, ("dp", "expert"), split_axis=0, concat_axis=0, tiled=True)
    arrived_rows = arrived.reshape(worker_ordinal * slot_count, model_width)
    picked = jnp.take(arrived_rows, positions, axis=0)
    gate_act = jnp.dot(picked, w_gate[0], preferred_element_type=jnp.float32)
    up_act = jnp.dot(picked, w_up[0], preferred_element_type=jnp.float32)
    hidden = (jax.nn.silu(gate_act) * up_act).astype(jnp.bfloat16)
    result = jnp.dot(hidden, w_down[0], preferred_element_type=jnp.float32).astype(jnp.bfloat16)
    back_rows = (
        jnp.zeros((worker_ordinal * slot_count, model_width), jnp.bfloat16)
        .at[positions]
        .set(result)
    )
    returned = lax.all_to_all(
        back_rows.reshape(worker_ordinal, slot_count, model_width),
        ("dp", "expert"),
        split_axis=0,
        concat_axis=0,
        tiled=True,
    )
    summed = jnp.sum(
        returned.reshape(dp_count, expert_total, slot_count, model_width), axis=0, dtype=jnp.float32
    )
    placed = (jnp.arange(tok_count, dtype=jnp.int32)[:, None] == source_idx.reshape(1, -1)) & (
        present.reshape(1, -1) > 0
    )
    mixing = jnp.where(placed, weights.reshape(1, -1), 0.0)
    mixed = jnp.dot(
        mixing,
        summed.reshape(-1, model_width),
        precision=lax.Precision.HIGHEST,
        preferred_element_type=jnp.float32,
    )
    return mixed.astype(jnp.bfloat16)


def solution(mesh):
    in_specs = (
        P(("dp", "expert"), None),
        P(),
        P(),
        P("expert", None, "dp"),
        P("expert", None, "dp"),
        P("expert", "dp", None),
    )
    out_specs = P(("dp", "expert"), None)
    return jax.shard_map(shards, mesh=mesh, in_specs=in_specs, out_specs=out_specs, check_vma=False)
```

profile of v0, /device:TPU:29, one launch (start us, length us, event | category | flops | bytes accessed | tf_op | source)
XLA Modules:
  0.0 624.3 jit_solution(1905892311547333034)
XLA Ops:
  0.0 0.9 multiply_subtract_fusion
  0.9 0.7 broadcast_compare_fusion.1
  1.7 6.9 %reduce-window.6 = s32[8,32,3,128]{3,1,2,0:T(8,128)S(1)} reduce-window(s32[8,32,3,128]{3,1,2,0:T(8,128)S(1)} %copy_bitcast_fusion, s32[]{:T(128)} %constant.70.clone.1), window={size=1x1x1x128 pad=0_0x0_0x0_0x127_0}, to_apply=%region_0.1 | reduce-window | flops 12484608 | bytes 786436 | tf_op jit(solution)/shard_map/reduce-window
  8.6 0.2 slice.16
  8.8 0.2 copy.18
  9.1 0.2 bitcast_bitcast_fusion
  9.4 0.7 convert_reduce_fusion.1
  10.5 3.2 gather_fusion
  13.7 3.1 gather.11
  16.8 3.7 select_select_fusion
  20.5 7.2 %broadcast_in_dim.71 = bf16[4,8,18,7168]{3,2,1,0:T(8,128)(2,1)} broadcast(bf16[8,18,7168]{2,1,0:T(8,128)(2,1)} %select_select_fusion), dimensions={1,2,3} | broadcast | bytes 10321920 | tf_op jit(solution)/shard_map/broadcast_in_dim | solution.py:43
  27.7 6.2 all-to-all-start
  34.0 247.6 %all-to-all-done = bf16[32,18,7168]{2,1,0:T(8,128)(2,1)} async-done(((bf16[32,18,7168]{2,1,0:T(8,128)(2,1)}), bf16[32,18,7168]{2,1,0:T(8,128)(2,1)}, u32[]{:S(2)}, u32[]{:S(2)}) %all-to-all-start) | async-done | bytes 8257568 | tf_op jit(solution)/shard_map/all_to_all | solution.py:45
  281.6 10.5 %reshape.155 = bf16[576,7168]{1,0:T(8,128)(2,1)} reshape(bf16[32,18,7168]{2,1,0:T(8,128)(2,1)} %all-to-all-done) | data formatting | bytes 16515072 | tf_op jit(solution)/shard_map/reshape | solution.py:46
  292.1 17.1 %gather_fusion.1 = bf16[288,7168]{1,0:T(8,128)(2,1)} fusion(bf16[576,7168]{1,0:T(8,128)(2,1)} %reshape.155, s32[1024]{0:T(1024)S(1)} %pad_clamp_fusion), kind=kCustom, calls=%fused_computation.1 | custom fusion | bytes 8258688 | tf_op jit(solution)/shard_map/jit(_take)/gather | solution.py:47
  309.2 6.7 %fusion.3 = f32[288,512]{1,0:T(8,128)S(1)} fusion(bf16[1,7168,512]{2,1,0:T(8,128)(2,1)} %param.9, bf16[288,7168]{1,0:T(8,128)(2,1)} %gather_fusion.1, pred[288]{0:T(512)(128)(4,1)S(1)} %compare_and_fusion.1), kind=kOutput, calls=%fused_computation.9 | convolution fusion | flops 2115993600 | bytes 12058912 | tf_op jit(solution)/shard_map/dot_general | solution.py:48
  315.9 12.9 %convolution_convert_fusion = bf16[288,7168]{1,0:T(8,128)(2,1)} fusion(bf16[1,512,7168]{2,1,0:T(8,128)(2,1)} %param.11, bf16[1,7168,512]{2,1,0:T(8,128)(2,1)} %param.10, bf16[288,7168]{1,0:T(8,128)(2,1)} %gather_fusion.1, pred[288]{0:T(512)(128)(4,1)S(1)} %compare_and_fusion.1, f32[288,512]{1,0:T(8,128)S(1)} %fusion.3), kind=kOutput, calls=%fused_computation.4 | convolution fusion | flops 4232871936 | bytes 23527712 | tf_op jit(solution)/shard_map/dot_general | solution.py:51
  328.8 12.1 %scatter_custom_fusion = bf16[576,7168]{1,0:T(8,128)(2,1)} fusion(s32[288]{0:T(512)S(1)} %fusion.35, bf16[288,7168]{1,0:T(8,128)(2,1)} %convolution_convert_fusion, bf16[]{:T(256)} %constant.81.clone.1), kind=kCustom, calls=%fused_computation.11 | custom fusion | bytes 8258048 | tf_op jit(solution)/shard_map/scatter | solution.py:55
  341.0 10.4 %reshape.156 = bf16[32,18,7168]{2,1,0:T(8,128)(2,1)} reshape(bf16[576,7168]{1,0:T(8,128)(2,1)} %scatter_custom_fusion) | data formatting | bytes 16515072 | tf_op jit(solution)/shard_map/reshape | solution.py:58
  351.3 5.1 all-to-all-start.1
  356.9 247.2 %all-to-all-done.1 = bf16[32,18,7168]{2,1,0:T(8,128)(2,1)} async-done(((bf16[32,18,7168]{2,1,0:T(8,128)(2,1)}), bf16[32,18,7168]{2,1,0:T(8,128)(2,1)}, u32[]{:S(2)}, u32[]{:S(2)}) %all-to-all-start.1) | async-done | bytes 8257568 | tf_op jit(solution)/shard_map/all_to_all | solution.py:57
  604.1 9.1 %convert_reduce_fusion = f32[8,18,7168]{2,1,0:T(8,128)} fusion(bf16[4,8,18,7168]{3,2,1,0:T(8,128)(2,1)} %bitcast.9), kind=kLoop, calls=%fused_computation.3 | loop fusion | flops 7225344 | bytes 12386304 | tf_op jit(solution)/shard_map/reduce_sum | solution.py:64
  613.1 4.3 reshape.157
  617.4 6.9 %convolution_convert_fusion.1 = bf16[128,7168]{1,0:T(8,128)(2,1)} fusion(f32[144,7168]{1,0:T(8,128)} %reshape.157, f32[144]{0:T(256)S(1)} %broadcast_in_dim.62, s32[144]{0:T(256)S(1)} %eq.66, pred[144]{0:T(512)(128)(4,1)S(1)} %gt.25), kind=kOutput, calls=%fused_computation.5 | convolution fusion | flops 1586419712 | bytes 5965072 | tf_op jit(solution)/shard_map/dot_general | solution.py:71
  (29 shorter events, 1.2 us)
Async XLA Ops:
  0.0 10.5 %copy-start = (bf16[128,7168]{1,0:T(8,128)(2,1)S(1)}, bf16[128,7168]{1,0:T(8,128)(2,1)}, u32[]{:S(2)}) copy-start(bf16[128,7168]{1,0:T(8,128)(2,1)} %param.6) | copy-start | bytes 5505028
  27.7 253.9 %all-to-all-start = ((bf16[32,18,7168]{2,1,0:T(8,128)(2,1)}), bf16[32,18,7168]{2,1,0:T(8,128)(2,1)}, u32[]{:S(2)}, u32[]{:S(2)}) async-start(bf16[32,18,7168]{2,1,0:T(8,128)(2,1)} %bitcast.38), calls=%async_computation | async-start | bytes 22020096 | tf_op jit(solution)/shard_map/all_to_all | solution.py:45
  351.3 5.2 copy-start.2
  351.3 252.7 %all-to-all-start.1 = ((bf16[32,18,7168]{2,1,0:T(8,128)(2,1)}), bf16[32,18,7168]{2,1,0:T(8,128)(2,1)}, u32[]{:S(2)}, u32[]{:S(2)}) async-start(bf16[32,18,7168]{2,1,0:T(8,128)(2,1)} %reshape.156), calls=%async_computation.1 | async-start | bytes 22020096 | tf_op jit(solution)/shard_map/all_to_all | solution.py:57
  613.1 11.2 %copy-start.1 = (bf16[128,7168]{1,0:T(8,128)(2,1)S(1)}, bf16[128,7168]{1,0:T(8,128)(2,1)}, u32[]{:S(2)}) copy-start(bf16[128,7168]{1,0:T(8,128)(2,1)} %param.6) | copy-start | bytes 5505028
where the time goes:
time: 625 us; the launch traced here: 624 us
  waiting for transfers between devices  495 us (79%)
  local copies, waits for them, and re-layouts  69 us (11%)
  matrix products  26.5 us (4%)
  other arithmetic  22.6 us (4%)
  starting transfers between devices  11.3 us (2%)
    all_to_all x1, waiting for transfers between devices, shards(): lax.all_to_all(spread, ('dp', 'expert'), split_axis=0, concat_axis=0, til...  248 us
    all_to_all x1, waiting for transfers between devices, shards(): lax.all_to_all(back_rows.reshape(worker_ordinal, slot_count, model_width)...  247 us
    gather x1, local copies, waits for them, and re-layouts, shards(): picked = jnp.take(arrived_rows, positions, axis=0)  17.1 us
    dot_general x1, matrix products, shards(): jnp.dot(hidden, w_down[0], preferred_element_type=jnp.float32)  12.9 us
  transfers between devices with their start and end apart: 2, of which 2 were waited for; matrix products, arithmetic and copies ran while one was open for 0% of the time, Pallas kernels for 0%

commit v1 on v0

v1 whole, which is shorter than its diff:
```python
import jax
import jax.numpy as jnp
from jax import lax
from jax.sharding import Mesh, PartitionSpec as P

BF = jnp.bfloat16
F32 = jnp.float32


def tables(chosen, combine_fixed, tok, dp, ea, eb):
    n = dp * ea * eb
    experts, cap = chosen.shape
    slot = min(tok, max(4, 2 * cap // n))
    r1 = -(-ea * slot // 16) * 16
    r2 = -(-dp * eb * slot // 16) * 16
    my_d, my_a, my_b = (lax.axis_index(k) for k in ("dp", "ea", "eb"))
    me = (my_d * ea + my_a) * eb + my_b
    owners = chosen // tok
    pos = jnp.arange(cap, dtype=jnp.int32)
    same = (owners[:, :, None] == owners[:, None, :]) & (pos[None, None, :] < pos[None, :, None])
    ranks = jnp.sum(same.astype(jnp.int32), axis=2)
    local = chosen - owners * tok
    match = ((owners == me)[:, None, :]) & (
        ranks[:, None, :] == jnp.arange(slot, dtype=jnp.int32)[None, :, None]
    )
    source = jnp.sum(jnp.where(match, local[:, None, :] + 1, 0), axis=2) - 1
    sel = (source[:, :, None] == jnp.arange(tok, dtype=jnp.int32)).astype(BF)
    sel = sel.reshape(ea, eb, slot, tok).transpose(1, 0, 2, 3).reshape(eb, ea * slot, tok)
    sel = jnp.pad(sel, ((0, 0), (0, r1 - ea * slot), (0, 0)))
    mine = my_a * eb + my_b
    own = lax.dynamic_index_in_dim(owners, mine, 0, keepdims=False)
    rank = lax.dynamic_index_in_dim(ranks, mine, 0, keepdims=False)
    weight = lax.dynamic_index_in_dim(combine_fixed, mine, 0, keepdims=False)
    weight = weight.astype(F32)[:, None] / 65536.0
    plane = (own // (ea * eb)) * eb + own % eb
    row_a = (own // eb) % ea
    where = plane * slot + rank
    pick = (row_a[None, :] == jnp.arange(ea, dtype=jnp.int32)[:, None])[:, :, None] & (
        where[None, :, None] == jnp.arange(r2, dtype=jnp.int32)
    )
    pick = pick.astype(BF)
    out_row = jnp.arange(r2, dtype=jnp.int32)[None, :, None]
    in_row = jnp.arange(dp * eb * r1, dtype=jnp.int32)[None, None, :]
    which = jnp.arange(ea, dtype=jnp.int32)[:, None, None]
    wanted = (out_row // slot) * r1 + which * slot + out_row % slot
    turn = ((in_row == wanted) & (out_row < dp * eb * slot)).astype(BF)
    return sel, pick, weight, turn, r1, r2


def dot(a, b):
    return jnp.dot(a, b, preferred_element_type=F32)


def shards(tokens, chosen, combine_fixed, w_gate, w_up, w_down):
    dp, ea, eb = (lax.axis_size(k) for k in ("dp", "ea", "eb"))
    tok, width = tokens.shape
    cap = chosen.shape[1]
    quarter = width // dp
    group = dp * eb
    sel, pick, weight, turn, r1, r2 = tables(chosen, combine_fixed, tok, dp, ea, eb)
    send = dot(sel.reshape(eb * r1, tok), tokens).astype(BF)
    send = send.reshape(eb, r1, dp, quarter).transpose(2, 0, 1, 3).reshape(group, r1, quarter)
    got = lax.all_to_all(send, ("dp", "eb"), 0, 0, tiled=True).reshape(group * r1, quarter)
    send = dot(turn.reshape(ea * r2, group * r1), got).astype(BF).reshape(ea, r2, quarter)
    got = lax.all_to_all(send, "ea", 0, 0, tiled=True).reshape(ea * r2, quarter)
    picked = dot(pick.transpose(1, 0, 2).reshape(cap, ea * r2), got).astype(BF)
    picked = lax.all_gather(picked, "dp", axis=1, tiled=True)
    gate = dot(picked, w_gate[0])
    up = dot(picked, w_up[0])
    hidden = (jax.nn.silu(gate) * up).astype(BF)
    part = dot(hidden, w_down[0]).astype(BF)
    total = lax.psum_scatter(part, "dp", scatter_dimension=1, tiled=True)
    total = (total.astype(F32) * weight).astype(BF)
    send = jnp.einsum("apr,pq->arq", pick, total, preferred_element_type=F32).astype(BF)
    got = lax.all_to_all(send, "ea", 0, 0, tiled=True)
    send = jnp.einsum("arg,arq->gq", turn, got, preferred_element_type=F32).astype(BF)
    got = lax.all_to_all(send.reshape(group, r1, quarter), ("dp", "eb"), 0, 0, tiled=True)
    mixed = jnp.einsum(
        "brt,dbrq->tdq", sel, got.reshape(dp, eb, r1, quarter), preferred_element_type=F32
    )
    return mixed.reshape(tok, width).astype(BF)


def solution(mesh):
    dp, experts = mesh.devices.shape
    finer = Mesh(mesh.devices.reshape(dp, experts // 2, 2), ("dp", "ea", "eb"))
    ex = ("ea", "eb")
    in_specs = (
        P(("dp",) + ex, None), P(), P(),
        P(ex, None, "dp"), P(ex, None, "dp"), P(ex, "dp", None),
    )
    return jax.shard_map(
        shards, mesh=finer, in_specs=in_specs, out_specs=P(("dp",) + ex, None), check_vma=False
    )
```

time: 625 us -> 321 us (0.51)
  waiting for transfers between devices: 495 us -> 194 us
  local copies, waits for them, and re-layouts: 69 us -> 16.3 us
  blocking collectives: 0 us -> 32.3 us
  other arithmetic: 22.6 us -> 4.29 us
  matrix products: 26.5 us -> 41 us
  between operations: 0.16 us -> 13.5 us
    all_to_all x2 -> x3, waiting for transfers between devices: 495 us -> 116 us  [the longest x1 45 us: shards(): got = lax.all_to_all(send, 'ea', 0, 0, tiled=True).reshape(ea * r2, quarter)]
    reduce_scatter x0 -> x1, waiting for transfers between devices: none -> 43.1 us  [shards(): total = lax.psum_scatter(part, 'dp', scatter_dimension=1, tiled=True)]
    all_gather x0 -> x1, waiting for transfers between devices: none -> 34.4 us  [shards(): picked = lax.all_gather(picked, 'dp', axis=1, tiled=True)]
    all_to_all x0 -> x1, blocking collectives: none -> 32.3 us  [shards(): lax.all_to_all(send.reshape(group, r1, quarter), ('dp', 'eb'), 0, 0, tile...]
    gather x3 -> x0, local copies, waits for them, and re-layouts: 23.5 us -> none  [the longest x1 17.1 us: shards(): picked = jnp.take(arrived_rows, positions, axis=0)]
    dot_general x3 -> x8, matrix products: 26.5 us -> 41 us  [the longest x5 29.9 us: dot(): return jnp.dot(a, b, preferred_element_type=F32)]
    reshape x4 -> x3, local copies, waits for them, and re-layouts: 25.3 us -> 11 us  [the longest x2 7.86 us: shards(): send.reshape(eb, r1, dp, quarter).transpose(2, 0, 1, 3)]
    scatter x1 -> x0, local copies, waits for them, and re-layouts: 12.1 us -> none  [shards(): back_rows = jnp.zeros((worker_ordinal * slot_count, model_width), jnp.bfl...]
  transfers between devices with their start and end apart: 2 -> 5, of which waited for: 2 -> 5; matrix products, arithmetic and copies ran while one was open for 0% -> 0% of each run, Pallas kernels for 0% -> 0%
where the time goes in v1:
time: 321 us; the launch traced here: 316 us
  waiting for transfers between devices  194 us (60%)
  matrix products  41 us (13%)
  blocking collectives  32.3 us (10%)
  local copies, waits for them, and re-layouts  16.3 us (5%)
  starting transfers between devices  14.4 us (4%)
  between operations  13.5 us (4%)
  other arithmetic  4.29 us (1%)
    all_to_all x1, waiting for transfers between devices, shards(): got = lax.all_to_all(send, 'ea', 0, 0, tiled=True).reshape(ea * r2, quarter)  45 us
    all_to_all x1, waiting for transfers between devices, shards(): got = lax.all_to_all(send, 'ea', 0, 0, tiled=True)  44.7 us
    reduce_scatter x1, waiting for transfers between devices, shards(): total = lax.psum_scatter(part, 'dp', scatter_dimension=1, tiled=True)  43.1 us
    all_gather x1, waiting for transfers between devices, shards(): picked = lax.all_gather(picked, 'dp', axis=1, tiled=True)  34.4 us
    all_to_all x1, blocking collectives, shards(): lax.all_to_all(send.reshape(group, r1, quarter), ('dp', 'eb'), 0, 0, tile...  32.3 us
    dot_general x5, matrix products, dot(): return jnp.dot(a, b, preferred_element_type=F32)  29.9 us
    all_to_all x1, waiting for transfers between devices, shards(): lax.all_to_all(send, ('dp', 'eb'), 0, 0, tiled=True)  26.6 us
    reshape x2, local copies, waits for them, and re-layouts, shards(): send.reshape(eb, r1, dp, quarter).transpose(2, 0, 1, 3)  7.86 us
  transfers between devices with their start and end apart: 5, of which 5 were waited for; matrix products, arithmetic and copies ran while one was open for 0% of the time, Pallas kernels for 0%

profile of v1, /device:TPU:29, one launch (start us, length us, event | category | flops | bytes accessed | tf_op | source)
XLA Modules:
  0.0 315.6 jit_solution(9152552151128663410)
XLA Ops:
  6.6 0.8 add_select_fusion
  8.2 1.3 convert_reduce_fusion
  10.1 2.1 convolution_convert_fusion.1
  12.2 4.6 %reshape.272 = bf16[2,80,4,1792]{3,2,1,0:T(4,128)(2,1)} reshape(bf16[160,7168]{1,0:T(8,128)(2,1)} %convolution_convert_fusion.1) | data formatting | bytes 4587520 | tf_op jit(solution)/shard_map/reshape | solution.py:62
  16.9 3.2 %copy.21 = bf16[2,80,4,1792]{3,1,0,2:T(8,128)(2,1)} copy(bf16[2,80,4,1792]{3,2,1,0:T(4,128)(2,1)} %reshape.272) | data formatting | bytes 4587520 | tf_op jit(solution)/shard_map/reshape | solution.py:62
  20.1 5.1 %all-to-all-start = ((bf16[8,80,1792]{2,1,0:T(8,128)(2,1)}), bf16[8,80,1792]{2,1,0:T(8,128)(2,1)}, u32[]{:S(2)}, u32[]{:S(2)}) async-start(bf16[8,80,1792]{2,1,0:T(8,128)(2,1)} %bitcast.52), calls=%async_computation | async-start | bytes 4587520 | tf_op jit(solution)/shard_map/all_to_all | solution.py:63
  25.7 26.6 %all-to-all-done = bf16[8,80,1792]{2,1,0:T(8,128)(2,1)} async-done(((bf16[8,80,1792]{2,1,0:T(8,128)(2,1)}), bf16[8,80,1792]{2,1,0:T(8,128)(2,1)}, u32[]{:S(2)}, u32[]{:S(2)}) %all-to-all-start) | async-done | bytes 2293792 | tf_op jit(solution)/shard_map/all_to_all | solution.py:63
  52.2 4.8 %convolution_convert_fusion.2 = bf16[576,1792]{1,0:T(8,128)(2,1)} fusion(bf16[640,1792]{1,0:T(8,128)(2,1)} %bitcast.5, s32[576]{0:T(1024)S(1)} %add_add_fusion, pred[576]{0:T(1024)(128)(4,1)S(1)} %and.139), kind=kOutput, calls=%fused_computation.11 | convolution fusion | flops 1322975232 | bytes 4361024 | tf_op jit(solution)/shard_map/dot_general | solution.py:51
  57.1 4.5 %all-to-all-start.1 = ((bf16[4,144,1792]{2,1,0:T(8,128)(2,1)}), bf16[4,144,1792]{2,1,0:T(8,128)(2,1)}, u32[]{:S(2)}, u32[]{:S(2)}) async-start(bf16[4,144,1792]{2,1,0:T(8,128)(2,1)} %bitcast.56), calls=%async_computation.1 | async-start | bytes 4128768 | tf_op jit(solution)/shard_map/all_to_all | solution.py:65
  61.7 45.0 %all-to-all-done.1 = bf16[4,144,1792]{2,1,0:T(8,128)(2,1)} async-done(((bf16[4,144,1792]{2,1,0:T(8,128)(2,1)}), bf16[4,144,1792]{2,1,0:T(8,128)(2,1)}, u32[]{:S(2)}, u32[]{:S(2)}) %all-to-all-start.1) | async-done | bytes 2064416 | tf_op jit(solution)/shard_map/all_to_all | solution.py:65
  106.8 3.6 %fusion.6 = bf16[288,1792]{1,0:T(8,128)(2,1)} fusion(bf16[4,144,1792]{2,1,0:T(8,128)(2,1)} %all-to-all-done.1, pred[288,144]{0,1:T(8,128)(4,1)S(1)} %iota_compare_fusion.3, pred[288,4]{0,1:T(4,128)(4,1)S(1)} %iota_compare_fusion.6), kind=kOutput, calls=%fused_computation.14 | convolution fusion | flops 595224576 | bytes 3139200 | tf_op jit(solution)/shard_map/dot_general | solution.py:51
  110.4 34.4 %all-gather.2.cloned.1.call-done = bf16[288,7168]{1,0:T(8,128)(2,1)} async-done(((bf16[288,1792]{1,0:T(8,128)(2,1)}), bf16[288,7168]{1,0:T(8,128)(2,1)}) %all-gather.2.cloned.1.call-update) | async-done | bytes 4128784 | tf_op jit(solution)/shard_map/all_gather | solution.py:67
  144.7 6.6 %fusion.4 = f32[288,512]{1,0:T(8,128)S(1)} fusion(bf16[288,7168]{1,0:T(8,128)(2,1)} %all-gather.2.cloned.1.call-done, bf16[1,7168,512]{2,1,0:T(8,128)(2,1)} %param.9), kind=kOutput, calls=%fused_computation.7 | convolution fusion | flops 2113929216 | bytes 12058624 | tf_op jit(solution)/shard_map/dot_general | solution.py:51
  151.4 12.8 %convolution_convert_fusion = bf16[288,7168]{1,0:T(8,128)(2,1)} fusion(bf16[1,512,7168]{2,1,0:T(8,128)(2,1)} %param.11, bf16[288,7168]{1,0:T(8,128)(2,1)} %all-gather.2.cloned.1.call-done, bf16[1,7168,512]{2,1,0:T(8,128)(2,1)} %param.10, f32[288,512]{1,0:T(8,128)S(1)} %fusion.4), kind=kOutput, calls=%fused_computation | convolution fusion | flops 4230807552 | bytes 23527424 | tf_op jit(solution)/shard_map/dot_general | solution.py:51
  164.2 0.7 multiply_reduce_fusion
  165.0 43.1 %reduce-scatter.2.cloned.1.call-done = bf16[288,1792]{1,0:T(8,128)(2,1)} async-done(((bf16[288,7168]{1,0:T(8,128)(2,1)}), bf16[288,1792]{1,0:T(8,128)(2,1)}) %reduce-scatter.2.cloned.1.call-update) | async-done | bytes 1032208 | tf_op jit(solution)/shard_map/reduce_scatter | solution.py:72
  208.1 3.9 %convolution_convert_fusion.3 = bf16[4,144,1792]{2,1,0:T(8,128)(2,1)} fusion(bf16[288,1792]{1,0:T(8,128)(2,1)} %reduce-scatter.2.cloned.1.call-done, f32[288]{0:T(512)S(1)} %multiply_reduce_fusion, pred[288,144]{0,1:T(8,128)(4,1)S(1)} %iota_compare_fusion.3, pred[4,288]{1,0:T(4,128)(4,1)S(1)} %iota_compare_fusion.7), kind=kOutput, calls=%fused_computation.12 | convolution fusion | flops 597288960 | bytes 3140352 | tf_op jit(solution)/shard_map/apr,pq->arq/dot_general | solution.py:74
  211.9 4.7 %all-to-all-start.2 = ((bf16[4,144,1792]{2,1,0:T(8,128)(2,1)}), bf16[4,144,1792]{2,1,0:T(8,128)(2,1)}, u32[]{:S(2)}, u32[]{:S(2)}) async-start(bf16[4,144,1792]{2,1,0:T(8,128)(2,1)} %convolution_convert_fusion.3), calls=%async_computation.3 | async-start | bytes 4128768 | tf_op jit(solution)/shard_map/all_to_all | solution.py:75
  216.7 44.7 %all-to-all-done.2 = bf16[4,144,1792]{2,1,0:T(8,128)(2,1)} async-done(((bf16[4,144,1792]{2,1,0:T(8,128)(2,1)}), bf16[4,144,1792]{2,1,0:T(8,128)(2,1)}, u32[]{:S(2)}, u32[]{:S(2)}) %all-to-all-start.2) | async-done | bytes 2064416 | tf_op jit(solution)/shard_map/all_to_all | solution.py:75
  261.5 3.7 %bitcast_convert_fusion = bf16[640,1792]{1,0:T(8,128)(2,1)S(1)} fusion(bf16[4,144,1792]{2,1,0:T(8,128)(2,1)} %all-to-all-done.2, s32[4,144]{1,0:T(4,128)S(1)} %add_add_fusion.1, pred[144]{0:T(512)(128)(4,1)S(1)} %iota_compare_fusion.8), kind=kOutput, calls=%fused_computation.9 | convolution fusion | flops 1323089920 | bytes 4360592 | tf_op jit(solution)/shard_map/arg,arq->gq/dot_general | solution.py:76
  265.1 32.3 %all_to_all.20 = bf16[8,80,1792]{2,1,0:T(8,128)(2,1)S(1)} all-to-all(bf16[8,80,1792]{2,1,0:T(8,128)(2,1)S(1)} %bitcast.55), channel_id=1, replica_groups=mesh['dp'=4,'ea'=4,'eb'=2] {'dp','eb'}, dimensions={0} | all-to-all | bytes 4587520 | tf_op jit(solution)/shard_map/all_to_all | solution.py:77
  297.4 3.2 %copy.24 = bf16[4,2,80,1792]{3,0,2,1:T(4,128)(2,1)} copy(bf16[4,2,80,1792]{3,2,1,0:T(8,128)(2,1)S(1)} %bitcast.53) | data formatting | bytes 4587520 | tf_op jit(solution)/shard_map/reshape | solution.py:79
  300.6 4.6 %dot_general.40 = bf16[7168,2,80]{0,2,1:T(8,128)(2,1)} reshape(bf16[4,1792,2,80]{1,0,3,2:T(4,128)(2,1)} %bitcast.54) | data formatting | bytes 4587520 | tf_op jit(solution)/shard_map/brt,dbrq->tdq/dot_general | solution.py:78
  305.2 3.6 %fusion = bf16[128,7168]{1,0:T(8,128)(2,1)} fusion(bf16[7168,2,80]{0,2,1:T(8,128)(2,1)} %dot_general.40, pred[2,72,128]{2,1,0:T(8,128)(4,1)S(1)} %iota_compare_fusion.5), kind=kOutput, calls=%fused_computation.3 | convolution fusion | flops 294518784 | bytes 4147200 | tf_op jit(solution)/shard_map/brt,dbrq->tdq/dot_general | solution.py:78
  (33 shorter events, 2.2 us)
Async XLA Ops:
  6.5 3.6 %copy-start = (bf16[128,7168]{1,0:T(8,128)(2,1)S(1)}, bf16[128,7168]{1,0:T(8,128)(2,1)}, u32[]{:S(2)}) copy-start(bf16[128,7168]{1,0:T(8,128)(2,1)} %param.6) | copy-start | bytes 5505028
  20.1 32.1 %all-to-all-start = ((bf16[8,80,1792]{2,1,0:T(8,128)(2,1)}), bf16[8,80,1792]{2,1,0:T(8,128)(2,1)}, u32[]{:S(2)}, u32[]{:S(2)}) async-start(bf16[8,80,1792]{2,1,0:T(8,128)(2,1)} %bitcast.52), calls=%async_computation | async-start | bytes 4587520 | tf_op jit(solution)/shard_map/all_to_all | solution.py:63
  57.1 49.7 %all-to-all-start.1 = ((bf16[4,144,1792]{2,1,0:T(8,128)(2,1)}), bf16[4,144,1792]{2,1,0:T(8,128)(2,1)}, u32[]{:S(2)}, u32[]{:S(2)}) async-start(bf16[4,144,1792]{2,1,0:T(8,128)(2,1)} %bitcast.56), calls=%async_computation.1 | async-start | bytes 4128768 | tf_op jit(solution)/shard_map/all_to_all | solution.py:65
  61.6 83.1 %all-gather.2.cloned.1.call-start = ((), (), s32[]{:S(2)}) async-start(), calls=%async_computation.5 | async-start | bytes 5160960 | tf_op jit(solution)/shard_map/all_gather | solution.py:67
  110.3 97.7 %reduce-scatter.2.cloned.1.call-start = ((), (), s32[]{:S(2)}) async-start(), calls=%async_computation.6 | async-start | bytes 5160960 | tf_op jit(solution)/shard_map/reduce_scatter | solution.py:72
  211.9 49.5 %all-to-all-start.2 = ((bf16[4,144,1792]{2,1,0:T(8,128)(2,1)}), bf16[4,144,1792]{2,1,0:T(8,128)(2,1)}, u32[]{:S(2)}, u32[]{:S(2)}) async-start(bf16[4,144,1792]{2,1,0:T(8,128)(2,1)} %convolution_convert_fusion.3), calls=%async_computation.3 | async-start | bytes 4128768 | tf_op jit(solution)/shard_map/all_to_all | solution.py:75
Sparse Core Ops, SparseCore 0:
  110.5 34.2 all-gather.1
  164.4 43.6 reduce-scatter.1

commit v2 on v1

--- a/solution.py
+++ b/solution.py
@@ -1,6 +1,10 @@
+import functools
+
 import jax
 import jax.numpy as jnp
 from jax import lax
+from jax.experimental import pallas as pl
+from jax.experimental.pallas import tpu as pltpu
 from jax.sharding import Mesh, PartitionSpec as P
 
 BF = jnp.bfloat16
@@ -51,34 +55,315 @@
     return jnp.dot(a, b, preferred_element_type=F32)
 
 
+def remote(src, dst, send_sem, recv_sem, target):
+    return pltpu.make_async_remote_copy(
+        src_ref=src, dst_ref=dst, send_sem=send_sem, recv_sem=recv_sem,
+        device_id=target, device_id_type=pl.DeviceIdType.MESH,
+    )
+
+
+def kernel(
+    dp, ea, eb, chunks,
+    tokens, sel, selt, pick, pickt, weight, turn, turnt, w_gate, w_up, w_down,
+    out,
+    wg, wu, wd, rows1, in1, in4, rows2, in2, in3, picked, gate, up, hidden,
+    pair_out, pair_in, far_out, far_in, total,
+    w_sem, s1, v1, s4, v4, s2, v2, s3, v3, s_far, s_pair, v_pick, s_sum, v_sum, s_ys, v_ys,
+):
+    d, a, b = (lax.axis_index(k) for k in ("dp", "ea", "eb"))
+    group = dp * eb
+    half = dp // 2
+    g = d * eb + b
+    sibling = d + 1 - 2 * lax.rem(d, 2)
+    cap, cols = total.shape[1:]
+
+    def peer(i):
+        p = lax.rem(g + i, group)
+        return p, (p // eb, a, lax.rem(p, eb))
+
+    def along(i):
+        e = lax.rem(a + i, ea)
+        return e, (d, e, b)
+
+    def far(j):
+        return lax.rem(d + 2 * j, dp)
+
+    def block(q, c):
+        return pl.ds(pl.multiple_of((q * chunks + c) * cols, 128), cols)
+
+    loads = [
+        pltpu.make_async_copy(src.at[0], dst, w_sem.at[k])
+        for k, (src, dst) in enumerate(((w_gate, wg), (w_up, wu), (w_down, wd)))
+    ]
+    for load in loads:
+        load.start()
+
+    barrier = pltpu.get_barrier_semaphore()
+
+    @pl.loop(1, group)
+    def _(i):
+        pl.semaphore_signal(barrier, inc=1, device_id=peer(i)[1], device_id_type=pl.DeviceIdType.MESH)
+
+    @pl.loop(1, ea)
+    def _(i):
+        pl.semaphore_signal(barrier, inc=1, device_id=along(i)[1], device_id_type=pl.DeviceIdType.MESH)
+
+    pl.semaphore_wait(barrier, group + ea - 2)
+
+    def sent1(c, i):
+        p, target = peer(i)
+        return remote(rows1.at[c, p], in1.at[c, g], s1.at[c, p], v1.at[c, g], target)
+
+    def came1(c, i):
+        p, target = peer(i)
+        return remote(rows1.at[c, p], in1.at[c, p], s1.at[c, p], v1.at[c, p], target)
+
+    for c in range(chunks):
+        @pl.loop(1, group)
+        def _(i):
+            p, _ = peer(i)
+            rows1[c, p] = dot(sel[lax.rem(p, eb)], tokens[:, block(p // eb, c)]).astype(BF)
+            sent1(c, i).start()
+
+        in1[c, g] = dot(sel[b], tokens[:, block(d, c)]).astype(BF)
+
+    def sent2(c, i):
+        e, target = along(i)
+        return remote(rows2.at[c, e], in2.at[c, a], s2.at[c, e], v2.at[c, a], target)
+
+    def came2(c, i):
+        e, target = along(i)
+        return remote(rows2.at[c, e], in2.at[c, e], s2.at[c, e], v2.at[c, e], target)
+
+    for c in range(chunks):
+        @pl.loop(1, group)
+        def _(i):
+            came1(c, i).wait_recv()
+
+        @pl.loop(1, ea)
+        def _(i):
+            e, _ = along(i)
+            rows2[c, e] = dot(turn[e], in1[c].reshape(-1, cols)).astype(BF)
+            sent2(c, i).start()
+
+        in2[c, a] = dot(turn[a], in1[c].reshape(-1, cols)).astype(BF)
+
+    def to_far(c, j):
+        mine = d * chunks + c
+        return remote(picked.at[mine], picked.at[mine], s_far.at[c, j], v_pick.at[mine], (far(j), a, b))
+
+    def to_pair(c, j):
+        slot = far(j) * chunks + c
+        return remote(picked.at[slot], picked.at[slot], s_pair.at[c, j], v_pick.at[slot], (sibling, a, b))
+
+    def arrival(q, c):
+        slot = q * chunks + c
+        return remote(picked.at[slot], picked.at[slot], s_pair.at[0, 0], v_pick.at[slot], (sibling, a, b))
+
+    def project(q, c):
+        slot = q * chunks + c
+        x = picked[slot]
+        where = pl.ds(pl.multiple_of(slot * cols, 128), cols)
+        gate[...] += dot(x, wg[where, :])
+        up[...] += dot(x, wu[where, :])
+
+    gate[...] = jnp.zeros_like(gate)
+    up[...] = jnp.zeros_like(up)
+    for c in range(chunks):
+        @pl.loop(1, ea)
+        def _(i):
+            came2(c, i).wait_recv()
+
+        x = dot(pick[0], in2[c, 0])
+        for e in range(1, ea):
+            x += dot(pick[e], in2[c, e])
+        picked[d * chunks + c] = x.astype(BF)
+
+        @pl.loop(1, half)
+        def _(j):
+            to_far(c, j).start()
+
+        to_pair(c, 0).start()
+    loads[0].wait()
+    loads[1].wait()
+
+    @pl.loop(0, chunks)
+    def _(c):
+        project(d, c)
+
+    @pl.loop(1, half)
+    def _(j):
+        @pl.loop(0, chunks)
+        def _(c):
+            arrival(far(j), c).wait_recv()
+            to_pair(c, j).start()
+            project(far(j), c)
+
+    @pl.loop(0, half)
+    def _(j):
+        @pl.loop(0, chunks)
+        def _(c):
+            q = lax.rem(sibling + 2 * j, dp)
+            arrival(q, c).wait_recv()
+            project(q, c)
+
+    v = gate[...]
+    hidden[...] = (v / (1.0 + jnp.exp(-v)) * up[...]).astype(BF)
+    loads[2].wait()
+
+    def pair_sum(c, j):
+        return remote(pair_out.at[c, j], pair_in.at[c, j], s_sum.at[c, j], v_sum.at[c, j], (sibling, a, b))
+
+    def far_sum(c, j):
+        return remote(far_out.at[c, j], far_in.at[c, j], s_ys.at[c, j], v_ys.at[c, j], (far(j), a, b))
+
+    def part(q, c):
+        return dot(hidden[...], wd[:, block(q, c)])
+
+    @pl.loop(1, half + 1)
+    def _(k):
+        j = lax.rem(k, half)
+
+        @pl.loop(0, chunks)
+        def _(c):
+            pair_out[c, j] = part(lax.rem(sibling + 2 * j, dp), c).astype(BF)
+            pair_sum(c, j).start()
+
+    @pl.loop(1, half)
+    def _(j):
+        @pl.loop(0, chunks)
+        def _(c):
+            mine = part(far(j), c)
+            pair_sum(c, j).wait_recv()
+            far_out[c, j] = (mine + pair_in[c, j].astype(F32)).astype(BF)
+            far_sum(c, j).start()
+
+    def sent3(c, i):
+        e, target = along(i)
+        return remote(rows2.at[c, e], in3.at[c, a], s3.at[c, e], v3.at[c, a], target)
+
+    def came3(c, i):
+        e, target = along(i)
+        return remote(rows2.at[c, e], in3.at[c, e], s3.at[c, e], v3.at[c, e], target)
+
+    for c in range(chunks):
+        mine = part(d, c)
+        pair_sum(c, 0).wait_recv()
+        mine += pair_in[c, 0].astype(F32)
+        for j in range(1, half):
+            far_sum(c, j).wait_recv()
+            mine += far_in[c, j].astype(F32)
+        total[c] = (mine * weight[...]).astype(BF)
+
+        @pl.loop(1, ea)
+        def _(i):
+            e, _ = along(i)
+            sent2(c, i).wait_send()
+            rows2[c, e] = dot(pickt[e], total[c]).astype(BF)
+            sent3(c, i).start()
+
+        in3[c, a] = dot(pickt[a], total[c]).astype(BF)
+
+    def sent4(c, i):
+        p, target = peer(i)
+        return remote(rows1.at[c, p], in4.at[c, g], s4.at[c, p], v4.at[c, g], target)
+
+    def came4(c, i):
+        p, target = peer(i)
+        return remote(rows1.at[c, p], in4.at[c, p], s4.at[c, p], v4.at[c, p], target)
+
+    for c in range(chunks):
+        @pl.loop(1, ea)
+        def _(i):
+            came3(c, i).wait_recv()
+
+        @pl.loop(1, group)
+        def _(i):
+            p, _ = peer(i)
+            sent1(c, i).wait_send()
+            rows1[c, p] = dot(turnt[p], in3[c].reshape(-1, cols)).astype(BF)
+            sent4(c, i).start()
+
+        in4[c, g] = dot(turnt[g], in3[c].reshape(-1, cols)).astype(BF)
+
+    for c in range(chunks):
+        @pl.loop(1, group)
+        def _(i):
+            came4(c, i).wait_recv()
+
+        @pl.loop(0, dp)
+        def _(q):
+            x = dot(selt[0], in4[c, q * eb])
+            for k in range(1, eb):
+                x += dot(selt[k], in4[c, q * eb + k])
+            out[:, block(q, c)] = x.astype(BF)
+
+    @pl.loop(0, chunks)
+    def _(c):
+        @pl.loop(1, group)
+        def _(i):
+            sent4(c, i).wait_send()
+
+        @pl.loop(1, ea)
+        def _(i):
+            sent3(c, i).wait_send()
+
+        @pl.loop(1, half)
+        def _(j):
+            to_far(c, j).wait_send()
+            far_sum(c, j).wait_send()
+
+        @pl.loop(0, half)
+        def _(j):
+            to_pair(c, j).wait_send()
+            pair_sum(c, j).wait_send()
+
+
 def shards(tokens, chosen, combine_fixed, w_gate, w_up, w_down):
     dp, ea, eb = (lax.axis_size(k) for k in ("dp", "ea", "eb"))
     tok, width = tokens.shape
     cap = chosen.shape[1]
+    units = w_gate.shape[2]
     quarter = width // dp
     group = dp * eb
+    half = dp // 2
+    chunks = 2 if quarter % 256 == 0 else 1
+    cols = quarter // chunks
     sel, pick, weight, turn, r1, r2 = tables(chosen, combine_fixed, tok, dp, ea, eb)
-    send = dot(sel.reshape(eb * r1, tok), tokens).astype(BF)
-    send = send.reshape(eb, r1, dp, quarter).transpose(2, 0, 1, 3).reshape(group, r1, quarter)
-    got = lax.all_to_all(send, ("dp", "eb"), 0, 0, tiled=True).reshape(group * r1, quarter)
-    send = dot(turn.reshape(ea * r2, group * r1), got).astype(BF).reshape(ea, r2, quarter)
-    got = lax.all_to_all(send, "ea", 0, 0, tiled=True).reshape(ea * r2, quarter)
-    picked = dot(pick.transpose(1, 0, 2).reshape(cap, ea * r2), got).astype(BF)
-    picked = lax.all_gather(picked, "dp", axis=1, tiled=True)
-    gate = dot(picked, w_gate[0])
-    up = dot(picked, w_up[0])
-    hidden = (jax.nn.silu(gate) * up).astype(BF)
-    part = dot(hidden, w_down[0]).astype(BF)
-    total = lax.psum_scatter(part, "dp", scatter_dimension=1, tiled=True)
-    total = (total.astype(F32) * weight).astype(BF)
-    send = jnp.einsum("apr,pq->arq", pick, total, preferred_element_type=F32).astype(BF)
-    got = lax.all_to_all(send, "ea", 0, 0, tiled=True)
-    send = jnp.einsum("arg,arq->gq", turn, got, preferred_element_type=F32).astype(BF)
-    got = lax.all_to_all(send.reshape(group, r1, quarter), ("dp", "eb"), 0, 0, tiled=True)
-    mixed = jnp.einsum(
-        "brt,dbrq->tdq", sel, got.reshape(dp, eb, r1, quarter), preferred_element_type=F32
-    )
-    return mixed.reshape(tok, width).astype(BF)
+    selt = sel.transpose(0, 2, 1)
+    pickt = pick.transpose(0, 2, 1)
+    turnt = turn.reshape(ea, r2, group, r1).transpose(2, 3, 0, 1).reshape(group, r1, ea * r2)
+    vmem = pl.BlockSpec(memory_space=pltpu.VMEM)
+    hbm = pl.BlockSpec(memory_space=pl.ANY)
+    sems = lambda *shape: pltpu.SemaphoreType.DMA(shape)
+    return pl.pallas_call(
+        functools.partial(kernel, dp, ea, eb, chunks),
+        out_shape=jax.ShapeDtypeStruct((tok, width), BF),
+        in_specs=[vmem] * 8 + [hbm] * 3,
+        out_specs=vmem,
+        scratch_shapes=[
+            pltpu.VMEM((width, units), BF), pltpu.VMEM((width, units), BF), pltpu.VMEM((units, width), BF),
+            pltpu.VMEM((chunks, group, r1, cols), BF),
+            pltpu.VMEM((chunks, group, r1, cols), BF),
+            pltpu.VMEM((chunks, group, r1, cols), BF),
+            pltpu.VMEM((chunks, ea, r2, cols), BF),
+            pltpu.VMEM((chunks, ea, r2, cols), BF),
+            pltpu.VMEM((chunks, ea, r2, cols), BF),
+            pltpu.VMEM((dp * chunks, cap, cols), BF),
+            pltpu.VMEM((cap, units), F32), pltpu.VMEM((cap, units), F32), pltpu.VMEM((cap, units), BF),
+            pltpu.VMEM((chunks, half, cap, cols), BF), pltpu.VMEM((chunks, half, cap, cols), BF),
+            pltpu.VMEM((chunks, half, cap, cols), BF), pltpu.VMEM((chunks, half, cap, cols), BF),
+            pltpu.VMEM((chunks, cap, cols), BF),
+            sems(3),
+            sems(chunks, group), sems(chunks, group), sems(chunks, group), sems(chunks, group),
+            sems(chunks, ea), sems(chunks, ea), sems(chunks, ea), sems(chunks, ea),
+            sems(chunks, half), sems(chunks, half), sems(dp * chunks),
+            sems(chunks, half), sems(chunks, half), sems(chunks, half), sems(chunks, half),
+        ],
+        compiler_params=pltpu.CompilerParams(
+            collective_id=0, has_side_effects=True, vmem_limit_bytes=62 * 1024 * 1024
+        ),
+    )(tokens, sel, selt, pick, pickt, weight, turn, turnt, w_gate, w_up, w_down)
 
 
 def solution(mesh):

time: 321 us -> 180 us (0.56); the launches traced: 316 us -> 178 us
  waiting for transfers between devices: 194 us -> 0 us
  Pallas kernels: 0 us -> 164 us
  matrix products: 41 us -> 0 us
  blocking collectives: 32.3 us -> 0 us
  starting transfers between devices: 14.4 us -> 0 us
  between operations: 13.5 us -> 0.08 us
  local copies, waits for them, and re-layouts: 16.3 us -> 4.71 us
  other arithmetic: 4.29 us -> 9.14 us
    pallas_call x0 -> x1, Pallas kernels: none -> 164 us  [shards(): pl.pallas_call(functools.partial(kernel, dp, ea, eb, chunks), out_shape=j...]
    all_to_all x3 -> x0, waiting for transfers between devices: 116 us -> none  [the longest x1 45 us: shards(): got = lax.all_to_all(send, 'ea', 0, 0, tiled=True).reshape(ea * r2, quarter)]
    reduce_scatter x1 -> x0, waiting for transfers between devices: 43.1 us -> none  [shards(): total = lax.psum_scatter(part, 'dp', scatter_dimension=1, tiled=True)]
    dot_general x8 -> x0, matrix products: 41 us -> none  [the longest x5 29.9 us: dot(): return jnp.dot(a, b, preferred_element_type=F32)]
    all_gather x1 -> x0, waiting for transfers between devices: 34.4 us -> none  [shards(): picked = lax.all_gather(picked, 'dp', axis=1, tiled=True)]
    all_to_all x1 -> x0, blocking collectives: 32.3 us -> none  [shards(): lax.all_to_all(send.reshape(group, r1, quarter), ('dp', 'eb'), 0, 0, tile...]
    all_to_all x3 -> x0, starting transfers between devices: 14.3 us -> none  [the longest x1 5.08 us: shards(): lax.all_to_all(send, ('dp', 'eb'), 0, 0, tiled=True)]
    reshape x3 -> x0, local copies, waits for them, and re-layouts: 11 us -> none  [the longest x2 7.86 us: shards(): send.reshape(eb, r1, dp, quarter).transpose(2, 0, 1, 3)]
  transfers between devices with their start and end apart: 5 -> 0, of which waited for: 5 -> 0; matrix products, arithmetic and copies ran while one was open for 0% -> 0% of each run, Pallas kernels for 0% -> 0%
where the time goes in v2:
time: 180 us; the launch traced here: 178 us
  Pallas kernels  164 us (91%)
  other arithmetic  9.14 us (5%)
  local copies, waits for them, and re-layouts  4.71 us (3%)
    pallas_call x1, Pallas kernels, shards(): pl.pallas_call(functools.partial(kernel, dp, ea, eb, chunks), out_shape=j...  164 us

profile of v2, /device:TPU:29, one launch (start us, length us, event | category | flops | bytes accessed | tf_op | source)
XLA Modules:
  0.0 178.3 jit_solution(6417255613870013629)
XLA Ops:
  0.0 0.1 and.141
  0.1 0.7 multiply_bitcast_fusion
  0.8 0.1 add_add_fusion
  0.9 0.7 broadcast_compare_fusion
  1.6 0.1 add.145
  1.7 0.7 add_select_fusion
  2.5 1.3 convert_reduce_fusion
  3.8 0.4 select_reduce_fusion
  4.2 0.1 copy.17
  4.3 0.1 eq.138
  4.5 0.1 iota_compare_fusion.2
  4.6 0.6 fusion.5
  5.2 0.7 copy.19.sel
  6.0 0.8 copy.20.weight
  6.8 0.9 and_convert_fusion.2.pickt
  7.6 1.1 and_convert_fusion.1.pick
  8.7 1.2 fusion.1.turn
  9.9 1.2 and_convert_fusion.turnt
  11.1 164.3 %shard_map.64 = bf16[128,7168]{1,0:T(8,128)(2,1)} custom-call(bf16[128,7168]{1,0:T(8,128)(2,1)} %tokens.1, bf16[2,80,128]{2,1,0:T(8,128)(2,1)} %copy.19.sel, bf16[2,128,80]{2,1,0:T(8,128)(2,1)} %get-tuple-element.7.selt, bf16[4,288,144]{2,1,0:T(8,128)(2,1)} %and_convert_fusion.1.pick, bf16[4,144,288]{2,1,0:T(8,128)(2,1)} %and_convert_fusion.2.pickt, ...), custom_call_target="tpu_custom_call" | custom-call | tf_op jit(solution)/shard_map/pallas_call | solution.py:339
  175.4 2.8 %copy.22 = bf16[128,7168]{1,0:T(8,128)(2,1)} copy(bf16[128,7168]{1,0:T(8,128)(2,1)} %shard_map.64) | data formatting | bytes 3670016
  (13 shorter events, 0.2 us)

commit v3 on v2

--- a/solution.py
+++ b/solution.py
@@ -2,6 +2,7 @@
 
 import jax
 import jax.numpy as jnp
+import numpy as np
 from jax import lax
 from jax.experimental import pallas as pl
 from jax.experimental.pallas import tpu as pltpu
@@ -43,11 +44,11 @@
         where[None, :, None] == jnp.arange(r2, dtype=jnp.int32)
     )
     pick = pick.astype(BF)
-    out_row = jnp.arange(r2, dtype=jnp.int32)[None, :, None]
-    in_row = jnp.arange(dp * eb * r1, dtype=jnp.int32)[None, None, :]
-    which = jnp.arange(ea, dtype=jnp.int32)[:, None, None]
+    out_row = np.arange(r2)[None, :, None]
+    in_row = np.arange(dp * eb * r1)[None, None, :]
+    which = np.arange(ea)[:, None, None]
     wanted = (out_row // slot) * r1 + which * slot + out_row % slot
-    turn = ((in_row == wanted) & (out_row < dp * eb * slot)).astype(BF)
+    turn = ((in_row == wanted) & (out_row < dp * eb * slot)).astype(np.float32)
     return sel, pick, weight, turn, r1, r2
 
 
@@ -118,7 +119,8 @@
         p, target = peer(i)
         return remote(rows1.at[c, p], in1.at[c, p], s1.at[c, p], v1.at[c, p], target)
 
-    for c in range(chunks):
+    @pl.loop(0, chunks)
+    def _(c):
         @pl.loop(1, group)
         def _(i):
             p, _ = peer(i)
@@ -135,7 +137,8 @@
         e, target = along(i)
         return remote(rows2.at[c, e], in2.at[c, e], s2.at[c, e], v2.at[c, e], target)
 
-    for c in range(chunks):
+    @pl.loop(0, chunks)
+    def _(c):
         @pl.loop(1, group)
         def _(i):
             came1(c, i).wait_recv()
@@ -167,9 +170,7 @@
         gate[...] += dot(x, wg[where, :])
         up[...] += dot(x, wu[where, :])
 
-    gate[...] = jnp.zeros_like(gate)
-    up[...] = jnp.zeros_like(up)
-    for c in range(chunks):
+    def pick_rows(c):
         @pl.loop(1, ea)
         def _(i):
             came2(c, i).wait_recv()
@@ -184,29 +185,35 @@
             to_far(c, j).start()
 
         to_pair(c, 0).start()
-    loads[0].wait()
-    loads[1].wait()
-
-    @pl.loop(0, chunks)
-    def _(c):
-        project(d, c)
-
-    @pl.loop(1, half)
-    def _(j):
-        @pl.loop(0, chunks)
-        def _(c):
+
+    def pass_on(c):
+        @pl.loop(1, half)
+        def _(j):
             arrival(far(j), c).wait_recv()
             to_pair(c, j).start()
             project(far(j), c)
 
-    @pl.loop(0, half)
-    def _(j):
-        @pl.loop(0, chunks)
-        def _(c):
+    def from_pair(c):
+        @pl.loop(0, half)
+        def _(j):
             q = lax.rem(sibling + 2 * j, dp)
             arrival(q, c).wait_recv()
             project(q, c)
 
+    gate[...] = jnp.zeros_like(gate)
+    up[...] = jnp.zeros_like(up)
+    for step in range(chunks + 2):
+        if step < chunks:
+            pick_rows(step)
+            if step == 0:
+                loads[0].wait()
+                loads[1].wait()
+            project(d, step)
+        if 1 <= step <= chunks:
+            pass_on(step - 1)
+        if step >= 2:
+            from_pair(step - 2)
+
     v = gate[...]
     hidden[...] = (v / (1.0 + jnp.exp(-v)) * up[...]).astype(BF)
     loads[2].wait()
@@ -220,19 +227,18 @@
     def part(q, c):
         return dot(hidden[...], wd[:, block(q, c)])
 
-    @pl.loop(1, half + 1)
-    def _(k):
-        j = lax.rem(k, half)
-
-        @pl.loop(0, chunks)
-        def _(c):
+    @pl.loop(0, chunks)
+    def _(c):
+        @pl.loop(1, half + 1)
+        def _(k):
+            j = lax.rem(k, half)
             pair_out[c, j] = part(lax.rem(sibling + 2 * j, dp), c).astype(BF)
             pair_sum(c, j).start()
 
-    @pl.loop(1, half)
-    def _(j):
-        @pl.loop(0, chunks)
-        def _(c):
+    @pl.loop(0, chunks)
+    def _(c):
+        @pl.loop(1, half)
+        def _(j):
             mine = part(far(j), c)
             pair_sum(c, j).wait_recv()
             far_out[c, j] = (mine + pair_in[c, j].astype(F32)).astype(BF)
@@ -246,7 +252,8 @@
         e, target = along(i)
         return remote(rows2.at[c, e], in3.at[c, e], s3.at[c, e], v3.at[c, e], target)
 
-    for c in range(chunks):
+    @pl.loop(0, chunks)
+    def _(c):
         mine = part(d, c)
         pair_sum(c, 0).wait_recv()
         mine += pair_in[c, 0].astype(F32)
@@ -272,7 +279,8 @@
         p, target = peer(i)
         return remote(rows1.at[c, p], in4.at[c, p], s4.at[c, p], v4.at[c, p], target)
 
-    for c in range(chunks):
+    @pl.loop(0, chunks)
+    def _(c):
         @pl.loop(1, ea)
         def _(i):
             came3(c, i).wait_recv()
@@ -286,7 +294,8 @@
 
         in4[c, g] = dot(turnt[g], in3[c].reshape(-1, cols)).astype(BF)
 
-    for c in range(chunks):
+    @pl.loop(0, chunks)
+    def _(c):
         @pl.loop(1, group)
         def _(i):
             came4(c, i).wait_recv()
@@ -327,12 +336,13 @@
     quarter = width // dp
     group = dp * eb
     half = dp // 2
-    chunks = 2 if quarter % 256 == 0 else 1
+    chunks = next(k for k in (7, 2, 1) if quarter % (128 * k) == 0)
     cols = quarter // chunks
     sel, pick, weight, turn, r1, r2 = tables(chosen, combine_fixed, tok, dp, ea, eb)
     selt = sel.transpose(0, 2, 1)
     pickt = pick.transpose(0, 2, 1)
     turnt = turn.reshape(ea, r2, group, r1).transpose(2, 3, 0, 1).reshape(group, r1, ea * r2)
+    turn, turnt = jnp.asarray(turn, BF), jnp.asarray(turnt, BF)
     vmem = pl.BlockSpec(memory_space=pltpu.VMEM)
     hbm = pl.BlockSpec(memory_space=pl.ANY)
     sems = lambda *shape: pltpu.SemaphoreType.DMA(shape)

time: 180 us -> 148 us (0.82)
  Pallas kernels: 164 us -> 135 us
  other arithmetic: 9.14 us -> 6.63 us
    pallas_call x1, Pallas kernels: 164 us -> 135 us  [shards(): pl.pallas_call(functools.partial(kernel, dp, ea, eb, chunks), out_shape=j...]
    convert_element_type x2 -> x0, other arithmetic: 2.4 us -> none  [tables(): turn = ((in_row == wanted) & (out_row < dp * eb * slot)).astype(BF)]
where the time goes in v3:
time: 148 us; the launch traced here: 146 us
  Pallas kernels  135 us (91%)
  other arithmetic  6.63 us (4%)
  local copies, waits for them, and re-layouts  4.51 us (3%)
    pallas_call x1, Pallas kernels, shards(): pl.pallas_call(functools.partial(kernel, dp, ea, eb, chunks), out_shape=j...  135 us

profile of v3, /device:TPU:29, one launch (start us, length us, event | category | flops | bytes accessed | tf_op | source)
XLA Modules:
  0.0 146.0 jit_solution(9195770397536176869)
XLA Ops:
  0.0 0.7 multiply_bitcast_fusion
  0.7 0.7 broadcast_compare_fusion
  1.4 0.7 add_select_fusion
  2.2 1.3 convert_reduce_fusion
  3.5 0.4 select_reduce_fusion
  3.9 0.1 copy.19
  4.0 0.1 eq.108
  4.2 0.1 iota_compare_fusion.1
  4.3 0.6 fusion.3
  4.9 0.7 copy.21.sel
  5.6 0.8 copy.22.weight
  6.4 0.9 and_convert_fusion.1.pickt
  7.3 1.0 and_convert_fusion.pick
  8.3 134.8 %shard_map.82 = bf16[128,7168]{1,0:T(8,128)(2,1)} custom-call(bf16[128,7168]{1,0:T(8,128)(2,1)} %tokens.1, bf16[2,80,128]{2,1,0:T(8,128)(2,1)} %copy.21.sel, bf16[2,128,80]{2,1,0:T(8,128)(2,1)} %get-tuple-element.7.selt, bf16[4,288,144]{2,1,0:T(8,128)(2,1)} %and_convert_fusion.pick, bf16[4,144,288]{2,1,0:T(8,128)(2,1)} %and_convert_fusion.1.pickt, ...), custom_call_target="tpu_custom_call" | custom-call | tf_op jit(solution)/shard_map/pallas_call | solution.py:349
  143.2 2.8 %copy.24 = bf16[128,7168]{1,0:T(8,128)(2,1)} copy(bf16[128,7168]{1,0:T(8,128)(2,1)} %shard_map.82) | data formatting | bytes 3670016
  (8 shorter events, 0.2 us)
